TPU v7x, 32 devices: a whole 2x2x4 slice. The times are simulated.
32 devices in a mesh: ka: 16 (over z, y, x), ta: 2 (over core).
Axes of the slice: x: 2, y: 2, z: 4, core: 2. Of those that a mesh axis runs over, the one named last changes fastest.
Arguments:
- sigma_history: bfloat16 [32, 1024, 256], P('ka', 'ta'), may hold values from -6 to 6
- time_basis: bfloat16 [1024, 64], P('ta'), may hold values from -0.75 to 0.75
- history_coef: bfloat16 [32, 128, 256], P('ka', 'ta'), may hold values from -6 to 6
- green_now: float32 [32, 256], P('ka'), may hold values from -6 to 6
- hamilton: float32 [32, 256], P('ka'), may hold values from -1.5 to 1.5
- panel_block: bfloat16 [32, 512, 512], P('ka', 'ta'), may hold values from -7 to 7
- panel_lengths: int32 [2], P('ta'), may hold values from 1 to 16, 24 in all
- owners: int32 [32, 1], P('ka'), may hold values from 0 to 3
- sketch: bfloat16 [4, 512, 64], P(None, 'ka'), may hold values from -6 to 6
Outputs:
- green_next: float32 [32, 256], P('ka')
- ortho_factor: float32 [32, 512, 64], P('ka', 'ta')
- coef_factor: float32 [32, 64, 512], P('ka', None, 'ta')
Inputs may be any that keep to these rules, and one draw needn't show every extreme that they name: `owners`: every compressor rank serves some k-point. `panel_lengths`: they sum to 24; the largest is 16.
All inputs are finite; a program needn't handle non-finite values. No bound on the sum of `panel_lengths` on one device may be relied on, other than what follows from the above.
Results may differ from a plain program's by a relative error of at most 0.0095.
Values may be sent and summed in bfloat16 or wider, within the bound.
A program may use at most 64 MiB of HBM per device.

v0:
```python
import math

import jax
import jax.numpy as jnp
from jax import lax
from jax.sharding import PartitionSpec as P

NO = 16
R = 64
PROW_DEV = 16


step_size = 0.25


def prefix(value, axis, join, neutral):
    count, mine = (lax.axis_size(axis), lax.axis_index(axis))
    pieces = lax.all_gather(value, axis)
    running = jnp.full_like(value, 0) + jnp.asarray(neutral, value.dtype)

    def step(position, running):
        longer = join(running, pieces[position])
        return jnp.where(position < mine, longer, running)

    return lax.fori_loop(0, count - 1, step, running)


def add_counts(earlier, later):
    return earlier + later


def compress_panels(sketched, tri_panel):
    gram = jnp.einsum("srq,srp->sqp", sketched, sketched, precision=lax.Precision.HIGHEST)
    gram_total = lax.psum(gram, "ta")
    lower_factor = jnp.linalg.cholesky(gram_total)
    ortho = lax.linalg.triangular_solve(
        lower_factor, sketched, left_side=False, lower=True, transpose_a=True
    )
    coeffs = jnp.einsum(
        "srq,src->sqc", ortho.astype(jnp.bfloat16), tri_panel, preferred_element_type=jnp.float32
    )
    coef_total = lax.psum_scatter(
        coeffs.astype(jnp.bfloat16), "ta", scatter_dimension=2, tiled=True
    ).astype(jnp.float32)
    return (ortho, coef_total)


def body(
    sigma_history,
    time_basis,
    history_coef,
    green_now,
    hamilton,
    panel_block,
    panel_lengths,
    owners,
    sketch,
):
    high = lax.Precision.HIGHEST
    ta_count = lax.axis_size("ta")
    k_local = green_now.shape[0]
    summed = jnp.einsum(
        "jr,kjo->kro", time_basis, sigma_history, preferred_element_type=jnp.float32
    )
    summed = summed.reshape(k_local, R, NO, NO)
    coef_local = history_coef.astype(jnp.float32).reshape(k_local, R, NO, NO)
    block_part = jnp.einsum("krac,krcd->kad", summed, coef_local, precision=high).reshape(
        k_local, NO * NO
    )
    integral = lax.psum(block_part, "ta").reshape(k_local, NO, NO)
    integral = integral / math.sqrt(NO * sigma_history.shape[1] * ta_count)
    green = green_now.reshape(k_local, NO, NO)
    hmat = hamilton.reshape(k_local, NO, NO)
    for repeat in range(2):
        left_prod = jnp.einsum("kac,kcd->kad", hmat, green, precision=high)
        right_prod = jnp.einsum("kac,kcd->kad", green, hmat, precision=high)
        green = green + step_size * (left_prod - right_prod + integral)
    green_next = green.reshape(k_local, NO * NO)
    starts = prefix(panel_lengths, "ta", add_counts, jnp.zeros((1,), jnp.int32))
    begin = starts[0]
    length = panel_lengths[0]
    slot_index = jnp.arange(PROW_DEV, dtype=jnp.int32)
    row_time = begin + slot_index
    live_rows = slot_index < length
    col_count = panel_block.shape[2]
    col_time = jnp.arange(col_count, dtype=jnp.int32) // NO - PROW_DEV // 2
    keep = live_rows[:, None, None] & (col_time[None, None, :] <= row_time[:, None, None])
    keep = jnp.broadcast_to(keep, (PROW_DEV, NO, col_count)).reshape(PROW_DEV * NO, col_count)
    tri_panel = jnp.where(keep[None], panel_block, jnp.zeros_like(panel_block))
    owner_ids = owners[:, 0]
    rank_count = sketch.shape[0]
    pick = (owner_ids[:, None] == jnp.arange(rank_count, dtype=jnp.int32)[None, :]).astype(
        jnp.bfloat16
    )
    chosen = jnp.einsum(
        "ks,scq->kcq",
        pick,
        lax.all_gather(sketch, "ka", axis=1, tiled=True),
        preferred_element_type=jnp.float32,
    ).astype(jnp.bfloat16)
    sketched = jnp.einsum("krc,kcq->krq", tri_panel, chosen, preferred_element_type=jnp.float32)
    ortho_factor, coef_factor = compress_panels(sketched, tri_panel)
    return (green_next, ortho_factor, coef_factor)


def solution(mesh):
    in_specs = (
        P("ka", "ta", None),
        P("ta", None),
        P("ka", "ta", None),
        P("ka", None),
        P("ka", None),
        P("ka", "ta", None),
        P("ta"),
        P("ka", None),
        P(None, "ka", None),
    )
    out_specs = (P("ka", None), P("ka", "ta", None), P("ka", None, "ta"))
    return jax.shard_map(body, mesh=mesh, in_specs=in_specs, out_specs=out_specs, check_vma=False)
```

profile of v0, /device:TPU:0, one launch (start us, length us, event | category | flops | bytes accessed | tf_op | source)
XLA Modules:
  0.0 99.9 jit_solution(17144964824040056498)
XLA Ops:
  8.0 0.6 dynamic-slice
  8.5 0.8 dynamic-update-slice.3
  9.3 1.9 %all-reduce = s32[2]{0:T(128)S(1)} all-reduce(s32[2]{0:T(128)S(1)} %dynamic-update-slice.3), channel_id=2, replica_groups=mesh['ka'=16,'ta'=2] {'ta'}, use_global_device_ids=true, to_apply=%add | all-reduce | flops 2 | bytes 16
  11.3 45.4 %all_gather.11 = bf16[4,512,64]{2,0,1:T(4,128)(2,1)S(1)} all-gather(bf16[4,32,64]{2,0,1:T(4,128)(2,1)S(1)} %copy.42), channel_id=1, replica_groups=mesh['ka'=16,'ta'=2] {'ka'}, dimensions={1}, use_global_device_ids=true | all-gather | bytes 278528 | tf_op jit(solution)/shard_map/all_gather | solution.py:98
  56.8 0.4 copy.43
  57.2 0.3 copy-done.8
  57.4 0.3 convolution_convert_fusion.1
  57.9 0.3 copy-done.7
  58.2 0.3 fusion.6
  58.5 0.3 fusion.27
  58.8 0.6 copy-done.3
  59.3 0.2 convolution_bitcast_fusion
  59.6 0.1 copy.37
  59.7 0.7 copy-done.2
  60.4 0.1 copy.38
  60.5 0.3 convolution_bitcast_fusion.2
  60.9 0.1 reshape.111
  61.0 3.5 %all-reduce.1 = (f32[2,256]{1,0:T(2,128)S(1)}, f32[2,64,64]{1,2,0:T(8,128)S(1)}) all-reduce(f32[2,256]{1,0:T(2,128)S(1)} %reshape.111, f32[2,64,64]{1,2,0:T(8,128)S(1)} %fusion.27), channel_id=1, replica_groups=mesh['ka'=16,'ta'=2] {'ta'}, use_global_device_ids=true, to_apply=%region_0.0 | all-reduce | flops 8704 | bytes 69632 | tf_op jit(solution)/shard_map/psum | solution.py:70
  64.6 11.7 %custom-call.7 = f32[2,64,64]{2,1,0:T(8,128)S(1)} custom-call(f32[2,64,64]{2,1,0:T(8,128)S(1)} %fusion.13), custom_call_target="Cholesky" | custom-call | tf_op jit(solution)/shard_map/jit(cholesky)/cholesky | solution.py:35
  76.4 0.1 compare_reduce_fusion
  76.6 9.8 %custom-call.8 = f32[2,1,64,64]{2,3,1,0:T(8,128)S(1)} custom-call(f32[2,1,64,64]{3,2,1,0:T(8,128)S(1)} %select_bitcast_fusion), custom_call_target="InvertDiagBlocksLowerTriangular" | custom-call | tf_op jit(solution)/shard_map/triangular_solve | solution.py:36
  86.4 0.3 fusion.11
  86.8 0.9 convolution_convert_fusion
  87.8 0.6 copy-done.5
  88.5 0.6 copy-done.6
  89.1 0.1 fusion.26
  89.3 0.1 fusion.5
  89.4 0.2 convolution_bitcast_fusion.1
  89.6 0.1 fusion.2
  89.7 0.7 reshape.112
  90.4 1.1 %reduce-scatter.2.cloned.1.call-done = bf16[2,64,256]{2,1,0:T(8,128)(2,1)} async-done(((bf16[2,64,512]{2,1,0:T(8,128)(2,1)}), bf16[2,64,256]{2,1,0:T(8,128)(2,1)}) %reduce-scatter.2.cloned.1.call-update) | async-done | bytes 65552 | tf_op jit(solution)/shard_map/reduce_scatter | solution.py:42
  91.5 1.5 %convert_element_type.17 = f32[2,64,256]{2,1,0:T(8,128)} convert(bf16[2,64,256]{2,1,0:T(8,128)(2,1)} %reduce-scatter.2.cloned.1.call-done) | non-fusion elementwise | flops 32768 | bytes 196608 | tf_op jit(solution)/shard_map/convert_element_type | solution.py:44
  (33 shorter events, 0.7 us)
Async XLA Ops:
  7.2 51.6 %copy-start = (bf16[2,512,256]{2,1,0:T(8,128)(2,1)S(1)}, bf16[2,512,256]{2,1,0:T(8,128)(2,1)}, u32[]{:S(2)}) copy-start(bf16[2,512,256]{2,1,0:T(8,128)(2,1)} %param.9) | copy-start | bytes 1572868
  7.2 0.8 copy-start.9
  7.2 4.1 %copy-start.4 = (bf16[4,32,64]{2,1,0:T(8,128)(2,1)S(1)}, bf16[4,32,64]{2,1,0:T(8,128)(2,1)}, u32[]{:S(2)}) copy-start(bf16[4,32,64]{2,1,0:T(8,128)(2,1)} %param.17) | copy-start | bytes 49156
  7.2 84.3 %reduce-scatter.2.cloned.1.call-start = ((), (), s32[]{:S(2)}) async-start(), calls=%async_computation.1 | async-start | bytes 196608 | tf_op jit(solution)/shard_map/reduce_scatter | solution.py:42
  56.8 0.7 copy-start.8
  57.2 1.0 %copy-start.7 = (bf16[2,256,512]{2,1,0:T(8,128)(2,1)S(1)}, bf16[2,256,512]{2,1,0:T(8,128)(2,1)}, u32[]{:S(2)}) copy-start(bf16[2,256,512]{2,1,0:T(8,128)(2,1)} %param.14) | copy-start | bytes 1572868
  58.5 0.9 copy-start.3
  59.5 0.8 copy-start.2
  86.8 0.9 copy-start.1
  87.7 0.7 copy-start.5
  88.4 0.7 copy-start.6
Sparse Core Ops, SparseCore 0:
  87.8 3.6 reduce-scatter.1
where the time goes:
time: 100 us; the launch traced here: 99.9 us
  blocking collectives  50.9 us (51%)
  other arithmetic  23.4 us (23%)
  between operations  15 us (15%)
  local copies, waits for them, and re-layouts  6.15 us (6%)
  matrix products  3.23 us (3%)
  waiting for transfers between devices  1.12 us (1%)
    all_gather x1, blocking collectives, body(): lax.all_gather(sketch, 'ka', axis=1, tiled=True)  45.4 us
    another operation x4, other arithmetic, compress_panels(): lower_factor = jnp.linalg.cholesky(gram_total)  11.9 us
    another operation x3, other arithmetic, compress_panels(): lax.linalg.triangular_solve(lower_factor, sketched, left_side=False, lowe...  9.94 us
    unnamed x25, local copies, waits for them, and re-layouts  4.52 us
    psum x1, blocking collectives, body(): integral = lax.psum(block_part, 'ta').reshape(k_local, NO, NO)  3.54 us
  transfers between devices with their start and end apart: 1, of which 1 were waited for; matrix products, arithmetic and copies ran while one was open for 2% of the time, Pallas kernels for 0%

commit v1 on v0

v1 whole, which is shorter than its diff:
```python
import functools
import math

import jax
import jax.numpy as jnp
from jax import lax
from jax.experimental import pallas as pl
from jax.experimental.pallas import tpu as pltpu
from jax.sharding import PartitionSpec as P

MESH = pl.DeviceIdType.MESH
HIGH = lax.Precision.HIGHEST
F32 = jnp.float32
BF16 = jnp.bfloat16
STEP = 0.25
GROUP = 4


def iota(shape, dim):
    return lax.broadcasted_iota(jnp.int32, shape, dim)


def dot(a, b, da=1, db=0, precision=None):
    return lax.dot_general(
        a, b, (((da,), (db,)), ((), ())), precision=precision, preferred_element_type=F32
    )


def eliminate(mats, offsets, rank):
    count = rank // 8
    full = (8, mats[0].shape[1])
    sub = iota(full, 0)
    tiles = [[m[8 * i : 8 * i + 8] for i in range(count)] for m in mats]
    pivots = [[None] * count for _ in mats]
    for j in range(count):
        cols = [
            [
                [
                    jnp.broadcast_to(t[i][:, o + 8 * j + a : o + 8 * j + a + 1], full)
                    for a in range(8)
                ]
                for i in range(j, count)
            ]
            for t, o in zip(tiles, offsets)
        ]
        for n, t in enumerate(tiles):
            pivots[n][j] = jnp.ones(full, F32)
        for a in range(8):
            for n, t in enumerate(tiles):
                c = cols[n]
                pivot = jnp.broadcast_to(c[0][a][a : a + 1], full)
                inverse = 1.0 / pivot
                pivots[n][j] = jnp.where(sub == a, pivot, pivots[n][j])
                row = jnp.broadcast_to(t[j][a : a + 1], full)
                heads = [jnp.broadcast_to(c[0][b][a : a + 1], full) for b in range(a + 1, 8)]
                for i in range(j, count):
                    if i == j:
                        if a == 7:
                            continue
                        factor = jnp.where(sub > a, c[0][a] * inverse, 0.0)
                    else:
                        factor = c[i - j][a] * inverse
                    for b in range(a + 1, 8):
                        c[i - j][b] = c[i - j][b] - factor * heads[b - a - 1]
                    t[i] = t[i] - factor * row
    return [
        jnp.concatenate([x * lax.rsqrt(p) for x, p in zip(t, pv)], axis=0)
        for t, pv in zip(tiles, pivots)
    ]


def kernel(
    n_ka,
    n_ta,
    length_ref,
    start_ref,
    owner_ref,
    green_ref,
    ham_ref,
    sigma_hbm,
    basis_hbm,
    hist_hbm,
    panel_hbm,
    sketch_hbm,
    green_out,
    ortho_out,
    coef_out,
    sigma_ref,
    basis_ref,
    hist_ref,
    panel_ref,
    sketch_ref,
    packed,
    gathered,
    masked,
    part,
    parts,
    right,
    rights,
    local_sem,
    send1,
    recv1,
    send2,
    recv2,
    send3,
    recv3,
    send4,
    recv4,
):
    ka, ta = lax.axis_index("ka"), lax.axis_index("ta")
    k_local, rows, cols = panel_ref.shape
    rank = sketch_ref.shape[2]
    depth = sketch_ref.shape[1]
    ranks = sketch_ref.shape[0]
    share = ranks // 2 // n_ta
    oo = sigma_ref.shape[2]
    no = math.isqrt(oo)
    width = 2 * rank

    loads = [
        pltpu.make_async_copy(src, dst, local_sem.at[i])
        for i, (src, dst) in enumerate(
            [
                (sketch_hbm, sketch_ref),
                (panel_hbm, panel_ref),
                (basis_hbm, basis_ref),
                (sigma_hbm, sigma_ref),
                (hist_hbm, hist_ref),
            ]
        )
    ]
    for load in loads:
        load.start()

    barrier = pltpu.get_barrier_semaphore()
    for off in range(1, n_ka):
        pl.semaphore_signal(
            barrier, inc=1, device_id=(lax.rem(ka + off, n_ka), ta), device_id_type=MESH
        )
    for off in range(1, n_ta):
        pl.semaphore_signal(
            barrier, inc=1, device_id=(ka, lax.rem(ta + off, n_ta)), device_id_type=MESH
        )
    loads[0].wait()
    for pair in range(ranks // 2):
        packed[pair // share, pair % share] = jnp.concatenate(
            [sketch_ref[2 * pair], sketch_ref[2 * pair + 1]], axis=1
        )
    gathered[ta, ka] = packed[ta]
    pl.semaphore_wait(barrier, n_ka - 1 + n_ta - 1)

    first = []
    for off in range(n_ka - 1, 0, -1):
        to = lax.rem(ka + off, n_ka)
        copy = pltpu.make_async_remote_copy(
            src_ref=packed.at[ta],
            dst_ref=gathered.at[ta, ka],
            send_sem=send1.at[off],
            recv_sem=recv1.at[ka],
            device_id=(to, ta),
            device_id_type=MESH,
        )
        copy.start()
        first.append(copy)

    row = iota((rows, cols), 0)
    col = iota((rows, cols), 1)
    slot_row = lax.div(row, no) * no
    slots = rows // no
    keep = (col < (start_ref[0] + slots // 2 + 1) * no + slot_row) & (row < length_ref[0] * no)
    unit = jnp.where(keep, 1.0, 0.0).astype(BF16)
    loads[1].wait()
    for k in range(k_local):
        masked[k] = panel_ref[k] * unit

    gather_a = jnp.where(lax.div(iota((no, oo), 1), no) == iota((no, oo), 0), 1.0, 0.0)
    gather_d = jnp.where(
        lax.rem(iota((oo, no), 0), no) == iota((oo, no), 1), 1.0, 0.0
    )
    diag = lax.rem(iota((oo, oo), 0), no) == lax.div(iota((oo, oo), 1), no)
    for load in loads[2:]:
        load.wait()
    basis = basis_ref[...]
    for k in range(k_local):
        summed = dot(basis, sigma_ref[k])
        outer = dot(summed, hist_ref[k].astype(F32), 0, 0, HIGH)
        outer = jnp.where(diag, outer, 0.0)
        lane = iota((oo, width), 1) - (k % 2) * rank
        place = jnp.where(lax.rem(iota((oo, width), 0), no) == lane, 1.0, 0.0)
        piece = dot(dot(gather_a, outer, 1, 0, HIGH), place, 1, 0, HIGH)
        if k % 2 == 0:
            part[k // 2, rank:] = piece
        else:
            part[k // 2, rank:] = part[k // 2, rank:] + piece

    groups = n_ka // GROUP
    second = []
    mine = lax.div(ka, GROUP)
    for g in range(groups):
        group = lax.rem(mine + g, groups)
        for i in range(GROUP):
            source = group * GROUP + i

            @pl.when(source != ka)
            def _():
                pltpu.make_async_remote_copy(
                    src_ref=packed.at[ta],
                    dst_ref=gathered.at[ta, source],
                    send_sem=send1.at[0],
                    recv_sem=recv1.at[source],
                    device_id=(ka, lax.rem(ta + 1, n_ta)),
                    device_id_type=MESH,
                ).wait_recv()

        for off in range(1, n_ta):
            piece = gathered.at[ta, pl.ds(group * GROUP, GROUP)]
            copy = pltpu.make_async_remote_copy(
                src_ref=piece,
                dst_ref=piece,
                send_sem=send2.at[off, g],
                recv_sem=recv2.at[ta, group],
                device_id=(ka, lax.rem(ta + off, n_ta)),
                device_id_type=MESH,
            )
            copy.start()
            second.append(copy)
    for copy in first:
        copy.wait_send()
    for off in range(1, n_ta):
        source = lax.rem(ta + off, n_ta)
        for g in range(groups):
            piece = gathered.at[source, pl.ds(g * GROUP, GROUP)]
            pltpu.make_async_remote_copy(
                src_ref=piece,
                dst_ref=piece,
                send_sem=send2.at[off, g],
                recv_sem=recv2.at[source, g],
                device_id=(ka, source),
                device_id_type=MESH,
            ).wait_recv()

    sketched = []
    grams = []
    for k in range(k_local):
        owner = owner_ref[k]
        pair = lax.div(owner, 2)
        omega = gathered[lax.div(pair, share), :, lax.rem(pair, share)]
        both = dot(omega.reshape(n_ka * depth, width), masked[k], 0, 1)
        value = jnp.where(lax.rem(owner, 2) == 0, both[:rank], both[rank:])
        sketched.append(value)
        grams.append(dot(value, value, 1, 1, HIGH))
    for p in range(k_local // 2):
        part[p, :rank] = jnp.concatenate([grams[2 * p], grams[2 * p + 1]], axis=1)

    third = []
    for off in range(1, n_ta):
        copy = pltpu.make_async_remote_copy(
            src_ref=part,
            dst_ref=parts.at[ta],
            send_sem=send3.at[off],
            recv_sem=recv3.at[ta],
            device_id=(ka, lax.rem(ta + off, n_ta)),
            device_id_type=MESH,
        )
        copy.start()
        third.append(copy)
    for copy in second:
        copy.wait_send()
    for off in range(1, n_ta):
        source = lax.rem(ta + off, n_ta)
        pltpu.make_async_remote_copy(
            src_ref=part,
            dst_ref=parts.at[source],
            send_sem=send3.at[off],
            recv_sem=recv3.at[source],
            device_id=(ka, source),
            device_id_type=MESH,
        ).wait_recv()
    parts[ta] = part[...]
    total = parts[0]
    for b in range(1, n_ta):
        total = total + parts[b]

    lane = iota((rank, width), 1)
    line = iota((rank, width), 0)
    integrals = []
    for p in range(k_local // 2):
        gram = total[p, :rank]
        left = jnp.where(lane < rank, gram, jnp.where(lane == line + rank, 1.0, 0.0))
        other = jnp.where(lane >= rank, gram, jnp.where(lane == line, 1.0, 0.0))
        low, high = eliminate([left, other], [0, rank], rank)
        low = jnp.where(lane >= rank, low, 0.0)
        high = jnp.where(lane < rank, high, 0.0)
        empty = jnp.zeros((rank, rows), F32)
        low_st = jnp.concatenate([empty, sketched[2 * p]], axis=0)
        high_st = jnp.concatenate([sketched[2 * p + 1], empty], axis=0)
        ortho_out[2 * p] = dot(low, low_st, 1, 0, HIGH)
        ortho_out[2 * p + 1] = dot(high, high_st, 1, 0, HIGH)
        integrals += [total[p, rank:, :no], total[p, rank:, rank : rank + no]]

    block = cols // n_ta
    for k in range(k_local):
        value = dot(ortho_out[k].astype(BF16), masked[k]).astype(BF16)
        for b in range(n_ta):
            right[b, k] = value[:, b * block : (b + 1) * block]
    fourth = []
    for off in range(1, n_ta):
        to = lax.rem(ta + off, n_ta)
        copy = pltpu.make_async_remote_copy(
            src_ref=right.at[to],
            dst_ref=rights.at[ta],
            send_sem=send4.at[off],
            recv_sem=recv4.at[ta],
            device_id=(ka, to),
            device_id_type=MESH,
        )
        copy.start()
        fourth.append(copy)

    scale = 1.0 / math.sqrt(no * sigma_ref.shape[1] * n_ta)
    for k in range(k_local):
        integral = integrals[k] * scale
        green = dot(gather_a * green_ref[k : k + 1, :], gather_d, 1, 0, HIGH)
        ham = dot(gather_a * ham_ref[k : k + 1, :], gather_d, 1, 0, HIGH)
        for _ in range(2):
            turn = dot(ham, green, 1, 0, HIGH) - dot(green, ham, 1, 0, HIGH)
            green = green + STEP * (turn + integral)
        spread = dot(green, gather_d, 1, 1, HIGH) * gather_a
        green_out[k : k + 1, :] = jnp.sum(spread, axis=0, keepdims=True)

    for copy in third:
        copy.wait_send()
    for off in range(1, n_ta):
        source = lax.rem(ta + off, n_ta)
        pltpu.make_async_remote_copy(
            src_ref=right.at[0],
            dst_ref=rights.at[source],
            send_sem=send4.at[off],
            recv_sem=recv4.at[source],
            device_id=(ka, source),
            device_id_type=MESH,
        ).wait_recv()
    for k in range(k_local):
        value = right[ta, k].astype(F32)
        for off in range(1, n_ta):
            value = value + rights[lax.rem(ta + off, n_ta), k].astype(F32)
        coef_out[k] = value
    for copy in fourth:
        copy.wait_send()


def body(
    n_ka,
    n_ta,
    sigma_history,
    time_basis,
    history_coef,
    green_now,
    hamilton,
    panel_block,
    panel_lengths,
    owners,
    sketch,
):
    k_local, rows, cols = panel_block.shape
    ranks, depth, rank = sketch.shape
    oo = sigma_history.shape[2]
    no = math.isqrt(oo)
    share = ranks // 2 // n_ta
    groups = n_ka // GROUP
    if n_ta == 2:
        whole = cols // no - rows // no // 2
        starts = jnp.where(lax.axis_index("ta") == 0, 0, whole - panel_lengths)
    else:
        every = lax.all_gather(panel_lengths, "ta", tiled=True)
        earlier = jnp.arange(n_ta, dtype=jnp.int32) < lax.axis_index("ta")
        starts = jnp.sum(jnp.where(earlier, every, 0), keepdims=True)
    starts = starts.astype(jnp.int32)
    smem = pl.BlockSpec(memory_space=pltpu.SMEM)
    vmem = pl.BlockSpec(memory_space=pltpu.VMEM)
    hbm = pl.BlockSpec(memory_space=pl.ANY)
    dma = pltpu.SemaphoreType.DMA
    green, ortho, coef = pl.pallas_call(
        functools.partial(kernel, n_ka, n_ta),
        out_shape=(
            jax.ShapeDtypeStruct((k_local, oo), F32),
            jax.ShapeDtypeStruct((k_local, rank, rows), F32),
            jax.ShapeDtypeStruct((k_local, rank, cols // n_ta), F32),
        ),
        in_specs=[smem] * 3 + [vmem] * 2 + [hbm] * 5,
        out_specs=(vmem, vmem, vmem),
        scratch_shapes=[
            pltpu.VMEM(sigma_history.shape, BF16),
            pltpu.VMEM(time_basis.shape[::-1], BF16),
            pltpu.VMEM(history_coef.shape, BF16),
            pltpu.VMEM(panel_block.shape, BF16),
            pltpu.VMEM(sketch.shape, BF16),
            pltpu.VMEM((n_ta, share, depth, 2 * rank), BF16),
            pltpu.VMEM((n_ta, n_ka, share, depth, 2 * rank), BF16),
            pltpu.VMEM(panel_block.shape, BF16),
            pltpu.VMEM((k_local // 2, rank + no, 2 * rank), F32),
            pltpu.VMEM((n_ta, k_local // 2, rank + no, 2 * rank), F32),
            pltpu.VMEM((n_ta, k_local, rank, cols // n_ta), BF16),
            pltpu.VMEM((n_ta, k_local, rank, cols // n_ta), BF16),
            dma((5,)),
            dma((n_ka,)),
            dma((n_ka,)),
            dma((n_ta, groups)),
            dma((n_ta, groups)),
            dma((n_ta,)),
            dma((n_ta,)),
            dma((n_ta,)),
            dma((n_ta,)),
        ],
        compiler_params=pltpu.CompilerParams(
            collective_id=0, has_side_effects=True, vmem_limit_bytes=48 * 1024 * 1024
        ),
    )(
        panel_lengths,
        starts,
        owners.reshape(-1),
        green_now,
        hamilton,
        sigma_history,
        time_basis.T,
        history_coef,
        panel_block,
        sketch,
    )
    return green, ortho.transpose(0, 2, 1), coef


def solution(mesh):
    in_specs = (
        P("ka", "ta", None),
        P("ta", None),
        P("ka", "ta", None),
        P("ka", None),
        P("ka", None),
        P("ka", "ta", None),
        P("ta"),
        P("ka", None),
        P(None, "ka", None),
    )
    out_specs = (P("ka", None), P("ka", "ta", None), P("ka", None, "ta"))
    step = functools.partial(body, mesh.shape["ka"], mesh.shape["ta"])
    return jax.shard_map(step, mesh=mesh, in_specs=in_specs, out_specs=out_specs, check_vma=False)
```

time: 100 us -> 27.5 us (0.28)
  blocking collectives: 50.9 us -> 0 us
  other arithmetic: 23.4 us -> 0 us
  Pallas kernels: 0 us -> 18.7 us
  between operations: 15 us -> 1.33 us
  matrix products: 3.23 us -> 0 us
  waiting for transfers between devices: 1.12 us -> 0 us
    all_gather x1 -> x0, blocking collectives: 45.4 us -> none  [body(): lax.all_gather(sketch, 'ka', axis=1, tiled=True)]
    another operation x7 -> x0, other arithmetic: 21.8 us -> none  [the longest x4 11.9 us: compress_panels(): lower_factor = jnp.linalg.cholesky(gram_total)]
    pallas_call x0 -> x1, Pallas kernels: none -> 18.7 us  [body(): pl.pallas_call(functools.partial(kernel, n_ka, n_ta), out_shape=(jax.Shap...]
    psum x1 -> x0, blocking collectives: 3.54 us -> none  [body(): integral = lax.psum(block_part, 'ta').reshape(k_local, NO, NO)]
    dot_general x10 -> x0, matrix products: 2.91 us -> none  [the longest x1 0.88 us: compress_panels(): jnp.einsum('srq,src->sqc', ortho.astype(jnp.bfloat16), tri_panel, preferr...]
    unnamed x25 -> x19, local copies, waits for them, and re-layouts: 4.52 us -> 7.08 us
    unnamed x1 -> x0, blocking collectives: 1.92 us -> none
    convert_element_type x1 -> x0, other arithmetic: 1.5 us -> none  [compress_panels(): coef_total = lax.psum_scatter(coeffs.astype(jnp.bfloat16), 'ta', scatter_...]
  transfers between devices with their start and end apart: 1 -> 0, of which waited for: 1 -> 0; matrix products, arithmetic and copies ran while one was open for 2% -> 0% of each run, Pallas kernels for 0% -> 0%
where the time goes in v1:
time: 27.5 us; the launch traced here: 27.1 us
  Pallas kernels  18.7 us (68%)
  local copies, waits for them, and re-layouts  7.08 us (26%)
  between operations  1.33 us (5%)
    pallas_call x1, Pallas kernels, body(): pl.pallas_call(functools.partial(kernel, n_ka, n_ta), out_shape=(jax.Shap...  18.7 us
    unnamed x19, local copies, waits for them, and re-layouts  7.08 us

profile of v1, /device:TPU:0, one launch (start us, length us, event | category | flops | bytes accessed | tf_op | source)
XLA Modules:
  0.0 27.1 jit_solution(2595070211655009199)
XLA Ops:
  1.3 0.0 copy-start.6
  1.3 0.0 copy-start.5
  1.3 0.0 copy-start.7
  1.3 0.7 %copy-done.6 = f32[2,256]{1,0:T(2,128)S(1)} copy-done((f32[2,256]{1,0:T(2,128)S(1)}, f32[2,256]{1,0:T(2,128)}, u32[]{:S(2)}) %copy-start.6) | copy-done | bytes 2072
  2.0 0.0 copy-done.5
  2.0 0.0 copy-done.7
  2.0 0.0 copy-start
  2.0 1.0 %copy-done = bf16[2,512,256]{2,1,0:T(8,128)(2,1)S(1)} copy-done((bf16[2,512,256]{2,1,0:T(8,128)(2,1)S(1)}, bf16[2,512,256]{2,1,0:T(8,128)(2,1)}, u32[]{:S(2)}) %copy-start) | copy-done | bytes 524312
  3.0 0.0 copy-start.1
  3.0 1.0 %copy-done.1 = bf16[2,256,512]{2,1,0:T(8,128)(2,1)S(1)} copy-done((bf16[2,256,512]{2,1,0:T(8,128)(2,1)S(1)}, bf16[2,256,512]{2,1,0:T(8,128)(2,1)}, u32[]{:S(2)}) %copy-start.1) | copy-done | bytes 524312
  4.1 0.0 copy-start.2
  4.1 0.8 %copy-done.2 = bf16[512,64]{0,1:T(8,128)(2,1)S(1)} copy-done((bf16[512,64]{0,1:T(8,128)(2,1)S(1)}, bf16[512,64]{0,1:T(8,128)(2,1)}, u32[]{:S(2)}) %copy-start.2) | copy-done | bytes 65560
  4.9 0.0 copy-start.3
  4.9 0.8 %copy-done.3 = bf16[2,64,256]{2,1,0:T(8,128)(2,1)S(1)} copy-done((bf16[2,64,256]{2,1,0:T(8,128)(2,1)S(1)}, bf16[2,64,256]{2,1,0:T(8,128)(2,1)}, u32[]{:S(2)}) %copy-start.3) | copy-done | bytes 65560
  5.8 0.0 copy-start.4
  5.8 0.8 %copy-done.4 = bf16[4,32,64]{2,1,0:T(8,128)(2,1)S(1)} copy-done((bf16[4,32,64]{2,1,0:T(8,128)(2,1)S(1)}, bf16[4,32,64]{2,1,0:T(8,128)(2,1)}, u32[]{:S(2)}) %copy-start.4) | copy-done | bytes 16408
  6.5 18.7 %shard_map.112 = (f32[2,256]{1,0:T(2,128)S(1)}, f32[2,64,256]{2,1,0:T(8,128)S(1)}, f32[2,64,256]{2,1,0:T(8,128)S(1)}) custom-call(s32[1]{0:T(128)S(6)} %copy.15.length_ref, s32[1]{0:T(128)S(6)} %select_n.9.start_ref, s32[2]{0:T(128)S(1)} %bitcast.6, f32[2,256]{1,0:T(2,128)S(1)} %copy-done.5, f32[2,256]{1,0:T(2,128)S(1)} %copy-done.6, ...), custom_call_target="tpu_custom_call" | custom-call | tf_op jit(solution)/shard_map/pallas_call | solution.py:383
  25.2 0.6 %copy.16 = f32[2,256]{1,0:T(2,128)} copy(f32[2,256]{1,0:T(2,128)S(1)} %get-tuple-element.12) | data formatting | bytes 4096
  25.8 0.7 %copy.17 = f32[2,256,64]{1,2,0:T(8,128)} copy(f32[2,256,64]{1,2,0:T(8,128)S(1)} %bitcast.4) | data formatting | bytes 262144
  26.4 0.7 %copy.18 = f32[2,64,256]{2,1,0:T(8,128)} copy(f32[2,64,256]{2,1,0:T(8,128)S(1)} %get-tuple-element.14) | data formatting | bytes 262144
Async XLA Ops:
  1.3 0.7 %copy-start.6 = (f32[2,256]{1,0:T(2,128)S(1)}, f32[2,256]{1,0:T(2,128)}, u32[]{:S(2)}) copy-start(f32[2,256]{1,0:T(2,128)} %ham_ref.1) | copy-start | bytes 6148
  1.3 0.7 %copy-start.5 = (f32[2,256]{1,0:T(2,128)S(1)}, f32[2,256]{1,0:T(2,128)}, u32[]{:S(2)}) copy-start(f32[2,256]{1,0:T(2,128)} %green_ref.1) | copy-start | bytes 6148
  1.3 0.7 %copy-start.7 = (s32[2,1]{0,1:T(1,128)S(1)}, s32[2,1]{0,1:T(1,128)}, u32[]{:S(2)}) copy-start(s32[2,1]{0,1:T(1,128)} %param.16) | copy-start | bytes 28
  2.0 1.0 %copy-start = (bf16[2,512,256]{2,1,0:T(8,128)(2,1)S(1)}, bf16[2,512,256]{2,1,0:T(8,128)(2,1)}, u32[]{:S(2)}) copy-start(bf16[2,512,256]{2,1,0:T(8,128)(2,1)} %sigma_hbm.1) | copy-start | bytes 1572868
  3.0 1.0 %copy-start.1 = (bf16[2,256,512]{2,1,0:T(8,128)(2,1)S(1)}, bf16[2,256,512]{2,1,0:T(8,128)(2,1)}, u32[]{:S(2)}) copy-start(bf16[2,256,512]{2,1,0:T(8,128)(2,1)} %panel_hbm.1) | copy-start | bytes 1572868
  4.1 0.8 %copy-start.2 = (bf16[512,64]{0,1:T(8,128)(2,1)S(1)}, bf16[512,64]{0,1:T(8,128)(2,1)}, u32[]{:S(2)}) copy-start(bf16[512,64]{0,1:T(8,128)(2,1)} %param.10) | copy-start | bytes 196612
  4.9 0.8 %copy-start.3 = (bf16[2,64,256]{2,1,0:T(8,128)(2,1)S(1)}, bf16[2,64,256]{2,1,0:T(8,128)(2,1)}, u32[]{:S(2)}) copy-start(bf16[2,64,256]{2,1,0:T(8,128)(2,1)} %hist_hbm.1) | copy-start | bytes 196612
  5.8 0.8 %copy-start.4 = (bf16[4,32,64]{2,1,0:T(8,128)(2,1)S(1)}, bf16[4,32,64]{2,1,0:T(8,128)(2,1)}, u32[]{:S(2)}) copy-start(bf16[4,32,64]{2,1,0:T(8,128)(2,1)} %sketch_hbm.1) | copy-start | bytes 49156

commit v2 on v1

v2 whole, which is shorter than its diff:
```python
import functools
import math

import jax
import jax.numpy as jnp
from jax import lax
from jax.experimental import pallas as pl
from jax.experimental.pallas import tpu as pltpu
from jax.sharding import PartitionSpec as P

MESH = pl.DeviceIdType.MESH
HIGH = lax.Precision.HIGHEST
F32 = jnp.float32
BF16 = jnp.bfloat16
STEP = 0.25
GROUP = 4


def iota(shape, dim):
    return lax.broadcasted_iota(jnp.int32, shape, dim)


def dot(a, b, da=1, db=0, precision=None):
    return lax.dot_general(
        a, b, (((da,), (db,)), ((), ())), precision=precision, preferred_element_type=F32
    )


def eliminate(mats, offsets, rank):
    count = rank // 8
    full = (8, mats[0].shape[1])
    sub = iota(full, 0)
    tiles = [[m[8 * i : 8 * i + 8] for i in range(count)] for m in mats]
    rows_out = [[] for _ in mats]
    for j in range(count):
        cols = [
            [
                [
                    jnp.broadcast_to(t[i][:, o + 8 * j + a : o + 8 * j + a + 1], full)
                    for a in range(8)
                ]
                for i in range(j, count)
            ]
            for t, o in zip(tiles, offsets)
        ]
        heads = [c[0] for c in cols]
        pivot_rows = [t[j] for t in tiles]
        pivots = [jnp.ones(full, F32) for _ in mats]
        taken = [jnp.zeros(full, F32) for _ in mats]
        for a in range(8):
            for n in range(len(mats)):
                pivot = jnp.broadcast_to(heads[n][a][a : a + 1], full)
                inverse = pl.reciprocal(pivot, approx=False)
                pivots[n] = jnp.where(sub == a, pivot, pivots[n])
                taken[n] = jnp.where(sub == a, pivot_rows[n], taken[n])
                column = heads[n][a]
                for b in range(a + 1, 8):
                    head = heads[n][b]
                    scaled = jnp.broadcast_to(head[a : a + 1], full) * inverse
                    heads[n][b] = jnp.where(sub == a, scaled, head - column * scaled)
                rest = pivot_rows[n]
                scaled = jnp.broadcast_to(rest[a : a + 1], full) * inverse
                pivot_rows[n] = jnp.where(sub == a, scaled, rest - column * scaled)
        for n, t in enumerate(tiles):
            rows_out[n].append(taken[n] * lax.rsqrt(pivots[n]))
            if j + 1 == count:
                continue
            solved = [jnp.broadcast_to(pivot_rows[n][a : a + 1], full) for a in range(8)]
            for i in range(j + 1, count):
                terms = [cols[n][i - j][a] * solved[a] for a in range(8)]
                while len(terms) > 1:
                    terms = [terms[x] + terms[x + 1] for x in range(0, len(terms), 2)]
                t[i] = t[i] - terms[0]
    return [jnp.concatenate(r, axis=0) for r in rows_out]


def kernel(
    n_ka,
    n_ta,
    length_ref,
    owner_hbm,
    green_hbm,
    ham_hbm,
    sigma_hbm,
    basis_hbm,
    hist_hbm,
    panel_hbm,
    sketch_hbm,
    green_out,
    ortho_out,
    coef_out,
    owner_ref,
    green_ref,
    ham_ref,
    sigma_ref,
    basis_ref,
    hist_ref,
    panel_ref,
    sketch_ref,
    packed,
    gathered,
    masked,
    part,
    parts,
    local_sem,
    send1,
    recv1,
    send2,
    recv2,
    send3,
    recv3,
    send4,
    recv4,
):
    ka, ta = lax.axis_index("ka"), lax.axis_index("ta")
    unused, k_local, rows, cols = panel_ref.shape
    ranks, depth, rank = sketch_ref.shape
    share = ranks // 2 // n_ta
    oo = sigma_ref.shape[2]
    no = math.isqrt(oo)
    width = 2 * rank
    block = cols // n_ta

    loads = [
        pltpu.make_async_copy(src, dst, local_sem.at[i])
        for i, (src, dst) in enumerate(
            [
                (sketch_hbm, sketch_ref),
                (basis_hbm, basis_ref),
                (sigma_hbm, sigma_ref),
                (hist_hbm, hist_ref),
                (panel_hbm, panel_ref.at[0]),
                (owner_hbm, owner_ref),
                (green_hbm, green_ref),
                (ham_hbm, ham_ref),
            ]
        )
    ]
    for load in loads:
        load.start()

    barrier = pltpu.get_barrier_semaphore()
    for off in range(1, n_ka):
        pl.semaphore_signal(
            barrier, inc=1, device_id=(lax.rem(ka + off, n_ka), ta), device_id_type=MESH
        )
    for off in range(1, n_ta):
        pl.semaphore_signal(
            barrier, inc=1, device_id=(ka, lax.rem(ta + off, n_ta)), device_id_type=MESH
        )
    loads[0].wait()
    for pair in range(ranks // 2):
        packed[pair // share, pair % share] = jnp.concatenate(
            [sketch_ref[2 * pair], sketch_ref[2 * pair + 1]], axis=1
        )
    gathered[ta, ka] = packed[ta]
    pl.semaphore_wait(barrier, n_ka - 1 + n_ta - 1)

    first = []
    for off in range(n_ka - 1, 0, -1):
        to = lax.rem(ka + off, n_ka)
        copy = pltpu.make_async_remote_copy(
            src_ref=packed.at[ta],
            dst_ref=gathered.at[ta, ka],
            send_sem=send1.at[off],
            recv_sem=recv1.at[ka],
            device_id=(to, ta),
            device_id_type=MESH,
        )
        copy.start()
        first.append(copy)

    panels = []
    for off in range(1, n_ta):
        copy = pltpu.make_async_remote_copy(
            src_ref=panel_hbm,
            dst_ref=panel_ref.at[n_ta - off],
            send_sem=send4.at[off],
            recv_sem=recv4.at[n_ta - off],
            device_id=(ka, lax.rem(ta + off, n_ta)),
            device_id_type=MESH,
        )
        copy.start()
        panels.append(copy)

    gather_a = jnp.where(lax.div(iota((no, oo), 1), no) == iota((no, oo), 0), 1.0, 0.0)
    gather_d = jnp.where(lax.rem(iota((oo, no), 0), no) == iota((oo, no), 1), 1.0, 0.0)
    diag = lax.rem(iota((oo, oo), 0), no) == lax.div(iota((oo, oo), 1), no)
    for load in loads[1:4]:
        load.wait()
    basis = basis_ref[...]
    for k in range(k_local):
        summed = dot(basis, sigma_ref[k])
        outer = dot(summed, hist_ref[k].astype(F32), 0, 0, HIGH)
        outer = jnp.where(diag, outer, 0.0)
        part[k] = dot(dot(gather_a, outer, 1, 0, HIGH), gather_d, 1, 0, HIGH)
    third = []
    for off in range(1, n_ta):
        copy = pltpu.make_async_remote_copy(
            src_ref=part,
            dst_ref=parts.at[n_ta - off],
            send_sem=send3.at[off],
            recv_sem=recv3.at[n_ta - off],
            device_id=(ka, lax.rem(ta + off, n_ta)),
            device_id_type=MESH,
        )
        copy.start()
        third.append(copy)

    slots = rows // no
    if n_ta == 2:
        mine = length_ref[0]
        whole = cols // no - slots // 2
        lengths = [mine, whole - mine]
        starts = [jnp.where(ta == 0, 0, whole - mine), jnp.where(ta == 0, mine, 0)]
    else:
        lengths, starts = [], []
        for off in range(n_ta):
            at = lax.rem(ta + off, n_ta)
            length, start = jnp.int32(0), jnp.int32(0)
            for b in range(n_ta):
                length = jnp.where(at == b, length_ref[b], length)
                start = start + jnp.where(b < at, length_ref[b], 0)
            lengths.append(length)
            starts.append(start)
    row = iota((rows, cols), 0)
    lead = iota((rows, cols), 1) - lax.div(row, no) * no

    def mask(off):
        keep = (lead < (starts[off] + slots // 2 + 1) * no) & (row < lengths[off] * no)
        unit = jnp.where(keep, 1.0, 0.0).astype(BF16)
        for k in range(k_local):
            masked[off, k] = panel_ref[off, k] * unit

    loads[4].wait()
    mask(0)

    groups = n_ka // GROUP
    second = []
    home = lax.div(ka, GROUP)
    for g in range(groups):
        group = lax.rem(home + g, groups)
        for i in range(GROUP):
            source = group * GROUP + i

            @pl.when(source != ka)
            def _():
                pltpu.make_async_remote_copy(
                    src_ref=packed.at[ta],
                    dst_ref=gathered.at[ta, source],
                    send_sem=send1.at[0],
                    recv_sem=recv1.at[source],
                    device_id=(ka, lax.rem(ta + 1, n_ta)),
                    device_id_type=MESH,
                ).wait_recv()

        for off in range(1, n_ta):
            piece = gathered.at[ta, pl.ds(group * GROUP, GROUP)]
            copy = pltpu.make_async_remote_copy(
                src_ref=piece,
                dst_ref=piece,
                send_sem=send2.at[off, g],
                recv_sem=recv2.at[ta, group],
                device_id=(ka, lax.rem(ta + off, n_ta)),
                device_id_type=MESH,
            )
            copy.start()
            second.append(copy)

    for load in loads[5:]:
        load.wait()
    for off in range(1, n_ta):
        pltpu.make_async_remote_copy(
            src_ref=panel_hbm,
            dst_ref=panel_ref.at[off],
            send_sem=send4.at[off],
            recv_sem=recv4.at[off],
            device_id=(ka, lax.rem(ta + off, n_ta)),
            device_id_type=MESH,
        ).wait_recv()
        mask(off)
        pltpu.make_async_remote_copy(
            src_ref=part,
            dst_ref=parts.at[off],
            send_sem=send3.at[off],
            recv_sem=recv3.at[off],
            device_id=(ka, lax.rem(ta + off, n_ta)),
            device_id_type=MESH,
        ).wait_recv()

    for off in range(1, n_ta):
        source = lax.rem(ta + off, n_ta)
        for g in range(groups):
            piece = gathered.at[source, pl.ds(g * GROUP, GROUP)]
            pltpu.make_async_remote_copy(
                src_ref=piece,
                dst_ref=piece,
                send_sem=send2.at[off, g],
                recv_sem=recv2.at[source, g],
                device_id=(ka, source),
                device_id_type=MESH,
            ).wait_recv()

    sketched = []
    grams = []
    for k in range(k_local):
        owner = owner_ref[k]
        pair = lax.div(owner, 2)
        omega = gathered[lax.div(pair, share), :, lax.rem(pair, share)]
        omega = omega.reshape(n_ka * depth, width)
        values = []
        for off in range(n_ta):
            both = dot(omega, masked[off, k], 0, 1)
            values.append(jnp.where(lax.rem(owner, 2) == 0, both[:rank], both[rank:]))
        sketched.append(values)
        gram = dot(values[0], values[0], 1, 1, HIGH)
        for value in values[1:]:
            gram = gram + dot(value, value, 1, 1, HIGH)
        grams.append(gram)

    lane = iota((rank, width), 1)
    line = iota((rank, width), 0)
    inverses = []
    for p in range(k_local // 2):
        gram = jnp.concatenate([grams[2 * p], grams[2 * p + 1]], axis=1)
        left = jnp.where(lane < rank, gram, jnp.where(lane == line + rank, 1.0, 0.0))
        other = jnp.where(lane >= rank, gram, jnp.where(lane == line, 1.0, 0.0))
        low, high = eliminate([left, other], [0, rank], rank)
        inverses += [jnp.where(lane >= rank, low, 0.0), jnp.where(lane < rank, high, 0.0)]

    empty = jnp.zeros((rank, rows), F32)
    mine = pl.ds(pl.multiple_of(ta * block, block), block)
    for k in range(k_local):
        total = jnp.zeros((rank, block), F32)
        for off in range(n_ta):
            value = sketched[k][off]
            stack = [empty, value] if k % 2 == 0 else [value, empty]
            ortho = dot(inverses[k], jnp.concatenate(stack, axis=0), 1, 0, HIGH)
            if off == 0:
                ortho_out[k] = ortho
            piece = dot(ortho.astype(BF16), masked[off, k, :, mine])
            total = total + piece.astype(BF16).astype(F32)
        coef_out[k] = total

    scale = 1.0 / math.sqrt(no * sigma_ref.shape[1] * n_ta)
    for k in range(k_local):
        integral = part[k]
        for off in range(1, n_ta):
            integral = integral + parts[off, k]
        integral = integral * scale
        green = dot(gather_a * green_ref[k : k + 1, :], gather_d, 1, 0, HIGH)
        ham = dot(gather_a * ham_ref[k : k + 1, :], gather_d, 1, 0, HIGH)
        for _ in range(2):
            turn = dot(ham, green, 1, 0, HIGH) - dot(green, ham, 1, 0, HIGH)
            green = green + STEP * (turn + integral)
        spread = dot(green, gather_d, 1, 1, HIGH) * gather_a
        green_out[k : k + 1, :] = jnp.sum(spread, axis=0, keepdims=True)

    for copy in first + second + third + panels:
        copy.wait_send()


def finish(green_ref, ortho_ref, coef_ref, green_hbm, ortho_hbm, coef_hbm, sem):
    moves = [
        pltpu.make_async_copy(coef_ref, coef_hbm, sem.at[0]),
        pltpu.make_async_copy(ortho_ref, ortho_hbm, sem.at[1]),
        pltpu.make_async_copy(green_ref, green_hbm, sem.at[2]),
    ]
    for move in moves:
        move.start()
    for move in moves:
        move.wait()


def body(
    n_ka,
    n_ta,
    sigma_history,
    time_basis,
    history_coef,
    green_now,
    hamilton,
    panel_block,
    panel_lengths,
    owners,
    sketch,
):
    k_local, rows, cols = panel_block.shape
    ranks, depth, rank = sketch.shape
    oo = sigma_history.shape[2]
    no = math.isqrt(oo)
    share = ranks // 2 // n_ta
    groups = n_ka // GROUP
    lengths = panel_lengths
    if n_ta > 2:
        lengths = lax.all_gather(panel_lengths, "ta", tiled=True)
    smem = pl.BlockSpec(memory_space=pltpu.SMEM)
    vmem = pl.BlockSpec(memory_space=pltpu.VMEM)
    hbm = pl.BlockSpec(memory_space=pltpu.HBM)
    dma = pltpu.SemaphoreType.DMA
    outs = (
        jax.ShapeDtypeStruct((k_local, oo), F32),
        jax.ShapeDtypeStruct((k_local, rank, rows), F32),
        jax.ShapeDtypeStruct((k_local, rank, cols // n_ta), F32),
    )
    results = pl.pallas_call(
        functools.partial(kernel, n_ka, n_ta),
        out_shape=outs,
        in_specs=[smem] + [hbm] * 8,
        out_specs=(vmem, vmem, vmem),
        scratch_shapes=[
            pltpu.SMEM((k_local,), jnp.int32),
            pltpu.VMEM(green_now.shape, F32),
            pltpu.VMEM(green_now.shape, F32),
            pltpu.VMEM(sigma_history.shape, BF16),
            pltpu.VMEM(time_basis.shape[::-1], BF16),
            pltpu.VMEM(history_coef.shape, BF16),
            pltpu.VMEM((n_ta,) + panel_block.shape, BF16),
            pltpu.VMEM(sketch.shape, BF16),
            pltpu.VMEM((n_ta, share, depth, 2 * rank), BF16),
            pltpu.VMEM((n_ta, n_ka, share, depth, 2 * rank), BF16),
            pltpu.VMEM((n_ta,) + panel_block.shape, BF16),
            pltpu.VMEM((k_local, no, no), F32),
            pltpu.VMEM((n_ta, k_local, no, no), F32),
            dma((8,)),
            dma((n_ka,)),
            dma((n_ka,)),
            dma((n_ta, groups)),
            dma((n_ta, groups)),
            dma((n_ta,)),
            dma((n_ta,)),
            dma((n_ta,)),
            dma((n_ta,)),
        ],
        compiler_params=pltpu.CompilerParams(
            collective_id=0, has_side_effects=True, vmem_limit_bytes=56 * 1024 * 1024
        ),
    )(
        lengths,
        *[
            pltpu.with_memory_space_constraint(x, pltpu.HBM)
            for x in (
                owners.reshape(-1),
                green_now,
                hamilton,
                sigma_history,
                time_basis.T,
                history_coef,
                panel_block,
                sketch,
            )
        ],
    )
    green, ortho, coef = pl.pallas_call(
        finish,
        out_shape=outs,
        in_specs=[vmem] * 3,
        out_specs=(hbm, hbm, hbm),
        scratch_shapes=[dma((3,))],
        compiler_params=pltpu.CompilerParams(vmem_limit_bytes=8 * 1024 * 1024),
    )(*results)
    return green, ortho.transpose(0, 2, 1), coef


def solution(mesh):
    in_specs = (
        P("ka", "ta", None),
        P("ta", None),
        P("ka", "ta", None),
        P("ka", None),
        P("ka", None),
        P("ka", "ta", None),
        P("ta"),
        P("ka", None),
        P(None, "ka", None),
    )
    out_specs = (P("ka", None), P("ka", "ta", None), P("ka", None, "ta"))
    step = functools.partial(body, mesh.shape["ka"], mesh.shape["ta"])
    return jax.shard_map(step, mesh=mesh, in_specs=in_specs, out_specs=out_specs, check_vma=False)
```

time: 27.5 us -> 23.4 us (0.85)
  the two profiles are of different devices: /device:TPU:0 before, /device:TPU:1 now
where the time goes in v2:
time: 23.4 us; the launch traced here: 23.2 us
  Pallas kernels  19.4 us (83%)
  local copies, waits for them, and re-layouts  2.48 us (11%)
  between operations  1.3 us (6%)
    pallas_call x1, Pallas kernels, body(): pl.pallas_call(functools.partial(kernel, n_ka, n_ta), out_shape=outs, in_...  18.7 us
    unnamed x6, local copies, waits for them, and re-layouts  2.48 us
    pallas_call x1, Pallas kernels, body(): pl.pallas_call(finish, out_shape=outs, in_specs=[vmem] * 3, out_specs=(hb...  0.72 us

profile of v2, /device:TPU:1, one launch (start us, length us, event | category | flops | bytes accessed | tf_op | source)
XLA Modules:
  0.0 23.2 jit_solution(1831662559069436616)
XLA Ops:
  1.3 18.7 %shard_map.112 = (f32[2,256]{1,0:T(2,128)}, f32[2,64,256]{2,1,0:T(8,128)}, f32[2,64,256]{2,1,0:T(8,128)}) custom-call(s32[1]{0:T(128)S(6)} %copy.12.length_ref, s32[2]{0:T(128)} %bitcast.4, f32[2,256]{1,0:T(2,128)} %green_hbm.1, f32[2,256]{1,0:T(2,128)} %ham_hbm.1, bf16[2,512,256]{2,1,0:T(8,128)(2,1)} %sigma_hbm.1, bf16[64,512]{1,0:T(8,128)(2,1)} %bitcast.3, ...), custom_call_target="tpu_custom_call" | custom-call | tf_op jit(solution)/shard_map/pallas_call | solution.py:406
  20.0 0.0 copy-start.2
  20.0 0.7 %copy-done.2 = f32[2,256]{1,0:T(2,128)S(1)} copy-done((f32[2,256]{1,0:T(2,128)S(1)}, f32[2,256]{1,0:T(2,128)}, u32[]{:S(2)}) %copy-start.2) | copy-done | bytes 2072
  20.6 0.0 copy-start
  20.6 0.9 %copy-done = f32[2,64,256]{2,1,0:T(8,128)S(1)} copy-done((f32[2,64,256]{2,1,0:T(8,128)S(1)}, f32[2,64,256]{2,1,0:T(8,128)}, u32[]{:S(2)}) %copy-start) | copy-done | bytes 131096
  21.5 0.0 copy-start.1
  21.5 0.9 %copy-done.1 = f32[2,64,256]{2,1,0:T(8,128)S(1)} copy-done((f32[2,64,256]{2,1,0:T(8,128)S(1)}, f32[2,64,256]{2,1,0:T(8,128)}, u32[]{:S(2)}) %copy-start.1) | copy-done | bytes 131096
  22.4 0.7 %shard_map.113 = (f32[2,256]{1,0:T(2,128)}, f32[2,64,256]{2,1,0:T(8,128)}, f32[2,64,256]{2,1,0:T(8,128)}) custom-call(f32[2,256]{1,0:T(2,128)S(1)} %copy-done.2, f32[2,64,256]{2,1,0:T(8,128)S(1)} %copy-done, f32[2,64,256]{2,1,0:T(8,128)S(1)} %copy-done.1), custom_call_target="tpu_custom_call" | custom-call | tf_op jit(solution)/shard_map/pallas_call | solution.py:454
Async XLA Ops:
  20.0 0.7 %copy-start.2 = (f32[2,256]{1,0:T(2,128)S(1)}, f32[2,256]{1,0:T(2,128)}, u32[]{:S(2)}) copy-start(f32[2,256]{1,0:T(2,128)} %get-tuple-element.9.green_ref) | copy-start | bytes 6148
  20.6 0.9 %copy-start = (f32[2,64,256]{2,1,0:T(8,128)S(1)}, f32[2,64,256]{2,1,0:T(8,128)}, u32[]{:S(2)}) copy-start(f32[2,64,256]{2,1,0:T(8,128)} %get-tuple-element.10.ortho_ref) | copy-start | bytes 393220
  21.5 0.9 %copy-start.1 = (f32[2,64,256]{2,1,0:T(8,128)S(1)}, f32[2,64,256]{2,1,0:T(8,128)}, u32[]{:S(2)}) copy-start(f32[2,64,256]{2,1,0:T(8,128)} %get-tuple-element.11.coef_ref) | copy-start | bytes 393220

commit v3 on v2

--- a/solution.py
+++ b/solution.py
@@ -24,6 +24,22 @@
     return lax.dot_general(
         a, b, (((da,), (db,)), ((), ())), precision=precision, preferred_element_type=F32
     )
+
+
+def halves(x):
+    high = x.astype(BF16)
+    return high, (x - high.astype(F32)).astype(BF16)
+
+
+def fold(x, no):
+    y = x[:, :128]
+    for i in range(1, x.shape[1] // 128):
+        y = y + x[:, 128 * i : 128 * (i + 1)]
+    shift = 64
+    while shift >= no:
+        y = y + pltpu.roll(y, shift, 1)
+        shift //= 2
+    return y
 
 
 def eliminate(mats, offsets, rank):
@@ -86,6 +102,9 @@
     hist_hbm,
     panel_hbm,
     sketch_hbm,
+    green_hbm_out,
+    ortho_hbm_out,
+    coef_hbm_out,
     green_out,
     ortho_out,
     coef_out,
@@ -103,6 +122,7 @@
     part,
     parts,
     local_sem,
+    out_sem,
     send1,
     recv1,
     send2,
@@ -170,7 +190,7 @@
         copy.start()
         first.append(copy)
 
-    panels = []
+    panels, moves = [], []
     for off in range(1, n_ta):
         copy = pltpu.make_async_remote_copy(
             src_ref=panel_hbm,
@@ -183,17 +203,16 @@
         copy.start()
         panels.append(copy)
 
-    gather_a = jnp.where(lax.div(iota((no, oo), 1), no) == iota((no, oo), 0), 1.0, 0.0)
-    gather_d = jnp.where(lax.rem(iota((oo, no), 0), no) == iota((oo, no), 1), 1.0, 0.0)
+    own = lax.div(iota((no, oo), 1), no) == iota((no, oo), 0)
     diag = lax.rem(iota((oo, oo), 0), no) == lax.div(iota((oo, oo), 1), no)
     for load in loads[1:4]:
         load.wait()
     basis = basis_ref[...]
     for k in range(k_local):
-        summed = dot(basis, sigma_ref[k])
-        outer = dot(summed, hist_ref[k].astype(F32), 0, 0, HIGH)
-        outer = jnp.where(diag, outer, 0.0)
-        part[k] = dot(dot(gather_a, outer, 1, 0, HIGH), gather_d, 1, 0, HIGH)
+        summed = jnp.concatenate(halves(dot(basis, sigma_ref[k])), axis=0)
+        coef = jnp.concatenate([hist_ref[k], hist_ref[k]], axis=0)
+        outer = jnp.where(diag, dot(summed, coef, 0, 0), 0.0)
+        part[k] = fold(jnp.sum(outer.reshape(no, no, oo), axis=1), no)
     third = []
     for off in range(1, n_ta):
         copy = pltpu.make_async_remote_copy(
@@ -288,6 +307,22 @@
             device_id_type=MESH,
         ).wait_recv()
 
+    scale = 1.0 / math.sqrt(no * sigma_ref.shape[1] * n_ta)
+    for k in range(k_local):
+        integral = part[k]
+        for off in range(1, n_ta):
+            integral = integral + parts[off, k]
+        integral = integral * scale
+        green = fold(jnp.where(own, green_ref[k : k + 1, :], 0.0), no)
+        ham = fold(jnp.where(own, ham_ref[k : k + 1, :], 0.0), no)
+        for _ in range(2):
+            turn = dot(ham[:, :no], green, 1, 0, HIGH) - dot(green[:, :no], ham, 1, 0, HIGH)
+            green = green + STEP * (turn + integral)
+        spread = jnp.where(own, jnp.concatenate([green] * (oo // 128), axis=1), 0.0)
+        green_out[k : k + 1, :] = jnp.sum(spread, axis=0, keepdims=True)
+    moves.append(pltpu.make_async_copy(green_out, green_hbm_out, out_sem.at[2 * k_local]))
+    moves[-1].start()
+
     for off in range(1, n_ta):
         source = lax.rem(ta + off, n_ta)
         for g in range(groups):
@@ -313,51 +348,45 @@
             both = dot(omega, masked[off, k], 0, 1)
             values.append(jnp.where(lax.rem(owner, 2) == 0, both[:rank], both[rank:]))
         sketched.append(values)
-        gram = dot(values[0], values[0], 1, 1, HIGH)
-        for value in values[1:]:
-            gram = gram + dot(value, value, 1, 1, HIGH)
-        grams.append(gram)
+        gram = jnp.zeros((width, width), F32)
+        for off in range(n_ta):
+            values[off] = jnp.concatenate(halves(values[off]), axis=0)
+            gram = gram + dot(values[off], values[off], 1, 1)
+        gram = gram[:rank] + gram[rank:]
+        grams.append(gram + pltpu.roll(gram, rank, 1))
 
     lane = iota((rank, width), 1)
     line = iota((rank, width), 0)
+    mats = [jnp.where(lane < rank, g, jnp.where(lane == line + rank, 1.0, 0.0)) for g in grams]
     inverses = []
-    for p in range(k_local // 2):
-        gram = jnp.concatenate([grams[2 * p], grams[2 * p + 1]], axis=1)
-        left = jnp.where(lane < rank, gram, jnp.where(lane == line + rank, 1.0, 0.0))
-        other = jnp.where(lane >= rank, gram, jnp.where(lane == line, 1.0, 0.0))
-        low, high = eliminate([left, other], [0, rank], rank)
-        inverses += [jnp.where(lane >= rank, low, 0.0), jnp.where(lane < rank, high, 0.0)]
-
-    empty = jnp.zeros((rank, rows), F32)
+    for inverse in eliminate(mats, [0] * k_local, rank):
+        inverse = jnp.where(lane >= rank, inverse, 0.0)
+        inverse = inverse + pltpu.roll(inverse, rank, 1)
+        inverses.append(jnp.concatenate(halves(inverse), axis=0))
+
     mine = pl.ds(pl.multiple_of(ta * block, block), block)
     for k in range(k_local):
         total = jnp.zeros((rank, block), F32)
         for off in range(n_ta):
-            value = sketched[k][off]
-            stack = [empty, value] if k % 2 == 0 else [value, empty]
-            ortho = dot(inverses[k], jnp.concatenate(stack, axis=0), 1, 0, HIGH)
+            ortho = dot(inverses[k], sketched[k][off])
+            ortho = ortho[:rank] + ortho[rank:]
             if off == 0:
                 ortho_out[k] = ortho
+                move = pltpu.make_async_copy(ortho_out.at[k], ortho_hbm_out.at[k], out_sem.at[k])
+                move.start()
+                moves.append(move)
             piece = dot(ortho.astype(BF16), masked[off, k, :, mine])
             total = total + piece.astype(BF16).astype(F32)
         coef_out[k] = total
-
-    scale = 1.0 / math.sqrt(no * sigma_ref.shape[1] * n_ta)
-    for k in range(k_local):
-        integral = part[k]
-        for off in range(1, n_ta):
-            integral = integral + parts[off, k]
-        integral = integral * scale
-        green = dot(gather_a * green_ref[k : k + 1, :], gather_d, 1, 0, HIGH)
-        ham = dot(gather_a * ham_ref[k : k + 1, :], gather_d, 1, 0, HIGH)
-        for _ in range(2):
-            turn = dot(ham, green, 1, 0, HIGH) - dot(green, ham, 1, 0, HIGH)
-            green = green + STEP * (turn + integral)
-        spread = dot(green, gather_d, 1, 1, HIGH) * gather_a
-        green_out[k : k + 1, :] = jnp.sum(spread, axis=0, keepdims=True)
+        place = k_local + k
+        move = pltpu.make_async_copy(coef_out.at[k], coef_hbm_out.at[k], out_sem.at[place])
+        move.start()
+        moves.append(move)
 
     for copy in first + second + third + panels:
         copy.wait_send()
+    for move in moves:
+        move.wait()
 
 
 def finish(green_ref, ortho_ref, coef_ref, green_hbm, ortho_hbm, coef_hbm, sem):
@@ -395,7 +424,6 @@
     if n_ta > 2:
         lengths = lax.all_gather(panel_lengths, "ta", tiled=True)
     smem = pl.BlockSpec(memory_space=pltpu.SMEM)
-    vmem = pl.BlockSpec(memory_space=pltpu.VMEM)
     hbm = pl.BlockSpec(memory_space=pltpu.HBM)
     dma = pltpu.SemaphoreType.DMA
     outs = (
@@ -407,8 +435,9 @@
         functools.partial(kernel, n_ka, n_ta),
         out_shape=outs,
         in_specs=[smem] + [hbm] * 8,
-        out_specs=(vmem, vmem, vmem),
+        out_specs=(hbm, hbm, hbm),
         scratch_shapes=[
+            *[pltpu.VMEM(x.shape, F32) for x in outs],
             pltpu.SMEM((k_local,), jnp.int32),
             pltpu.VMEM(green_now.shape, F32),
             pltpu.VMEM(green_now.shape, F32),
@@ -420,9 +449,10 @@
             pltpu.VMEM((n_ta, share, depth, 2 * rank), BF16),
             pltpu.VMEM((n_ta, n_ka, share, depth, 2 * rank), BF16),
             pltpu.VMEM((n_ta,) + panel_block.shape, BF16),
-            pltpu.VMEM((k_local, no, no), F32),
-            pltpu.VMEM((n_ta, k_local, no, no), F32),
+            pltpu.VMEM((k_local, no, 128), F32),
+            pltpu.VMEM((n_ta, k_local, no, 128), F32),
             dma((8,)),
+            dma((2 * k_local + 1,)),
             dma((n_ka,)),
             dma((n_ka,)),
             dma((n_ta, groups)),
@@ -454,11 +484,11 @@
     green, ortho, coef = pl.pallas_call(
         finish,
         out_shape=outs,
-        in_specs=[vmem] * 3,
+        in_specs=[hbm] * 3,
         out_specs=(hbm, hbm, hbm),
         scratch_shapes=[dma((3,))],
         compiler_params=pltpu.CompilerParams(vmem_limit_bytes=8 * 1024 * 1024),
-    )(*results)
+    )(*[pltpu.with_memory_space_constraint(x, pltpu.HBM) for x in results])
     return green, ortho.transpose(0, 2, 1), coef
 
 

time: 23.4 us -> 28 us (1.20)
  the two profiles are of different devices: /device:TPU:1 before, /device:TPU:0 now
where the time goes in v3:
time: 28 us; the launch traced here: 27.8 us
  Pallas kernels  26.6 us (95%)
  between operations  1.29 us (5%)
    pallas_call x1, Pallas kernels, body(): pl.pallas_call(functools.partial(kernel, n_ka, n_ta), out_shape=outs, in_...  17.4 us
    pallas_call x1, Pallas kernels, body(): pl.pallas_call(finish, out_shape=outs, in_specs=[hbm] * 3, out_specs=(hbm...  9.13 us

profile of v3, /device:TPU:0, one launch (start us, length us, event | category | flops | bytes accessed | tf_op | source)
XLA Modules:
  0.0 27.8 jit_solution(17006524588097111823)
XLA Ops:
  1.3 17.4 %shard_map.112 = (f32[2,256]{1,0:T(2,128)}, f32[2,64,256]{2,1,0:T(8,128)}, f32[2,64,256]{2,1,0:T(8,128)}) custom-call(s32[1]{0:T(128)S(6)} %copy.12.length_ref, s32[2]{0:T(128)} %bitcast.4, f32[2,256]{1,0:T(2,128)} %green_hbm.1, f32[2,256]{1,0:T(2,128)} %ham_hbm.1, bf16[2,512,256]{2,1,0:T(8,128)(2,1)} %sigma_hbm.1, bf16[64,512]{1,0:T(8,128)(2,1)} %bitcast.3, ...), custom_call_target="tpu_custom_call" | custom-call | tf_op jit(solution)/shard_map/pallas_call | solution.py:434
  18.7 9.1 %shard_map.113 = (f32[2,256]{1,0:T(2,128)}, f32[2,64,256]{2,1,0:T(8,128)}, f32[2,64,256]{2,1,0:T(8,128)}) custom-call(f32[2,256]{1,0:T(2,128)} %get-tuple-element.9.green_ref, f32[2,64,256]{2,1,0:T(8,128)} %get-tuple-element.10.ortho_ref, f32[2,64,256]{2,1,0:T(8,128)} %get-tuple-element.11.coef_ref), custom_call_target="tpu_custom_call" | custom-call | tf_op jit(solution)/shard_map/pallas_call | solution.py:484

commit v4 on v3

--- a/solution.py
+++ b/solution.py
@@ -13,7 +13,6 @@
 F32 = jnp.float32
 BF16 = jnp.bfloat16
 STEP = 0.25
-GROUP = 4
 
 
 def iota(shape, dim):
@@ -59,29 +58,36 @@
             ]
             for t, o in zip(tiles, offsets)
         ]
-        heads = [c[0] for c in cols]
-        pivot_rows = [t[j] for t in tiles]
-        pivots = [jnp.ones(full, F32) for _ in mats]
-        taken = [jnp.zeros(full, F32) for _ in mats]
+        count_of = range(len(mats))
+        block = [
+            [[jnp.broadcast_to(c[0][b][a : a + 1], full) for b in range(8)] for a in range(8)]
+            for c in cols
+        ]
+        rows = [[jnp.broadcast_to(t[j][a : a + 1], full) for a in range(8)] for t in tiles]
+        inverse = [[None] * 8 for _ in mats]
         for a in range(8):
-            for n in range(len(mats)):
-                pivot = jnp.broadcast_to(heads[n][a][a : a + 1], full)
-                inverse = pl.reciprocal(pivot, approx=False)
-                pivots[n] = jnp.where(sub == a, pivot, pivots[n])
-                taken[n] = jnp.where(sub == a, pivot_rows[n], taken[n])
-                column = heads[n][a]
+            for n in count_of:
+                v, r = block[n], rows[n]
+                inverse[n][a] = pl.reciprocal(v[a][a], approx=False)
                 for b in range(a + 1, 8):
-                    head = heads[n][b]
-                    scaled = jnp.broadcast_to(head[a : a + 1], full) * inverse
-                    heads[n][b] = jnp.where(sub == a, scaled, head - column * scaled)
-                rest = pivot_rows[n]
-                scaled = jnp.broadcast_to(rest[a : a + 1], full) * inverse
-                pivot_rows[n] = jnp.where(sub == a, scaled, rest - column * scaled)
+                    factor = v[a][b] * inverse[n][a]
+                    v[b][a] = factor
+                    for c in range(b, 8):
+                        v[b][c] = v[b][c] - factor * v[a][c]
+                    r[b] = r[b] - factor * r[a]
         for n, t in enumerate(tiles):
-            rows_out[n].append(taken[n] * lax.rsqrt(pivots[n]))
+            v, r = block[n], rows[n]
+            pivot, taken = v[7][7], r[7]
+            for a in range(7):
+                pivot = jnp.where(sub == a, v[a][a], pivot)
+                taken = jnp.where(sub == a, r[a], taken)
+            rows_out[n].append(taken * lax.rsqrt(pivot))
             if j + 1 == count:
                 continue
-            solved = [jnp.broadcast_to(pivot_rows[n][a : a + 1], full) for a in range(8)]
+            solved = [x * i for x, i in zip(r, inverse[n])]
+            for b in range(7, 0, -1):
+                for a in range(b):
+                    solved[a] = solved[a] - v[b][a] * solved[b]
             for i in range(j + 1, count):
                 terms = [cols[n][i - j][a] * solved[a] for a in range(8)]
                 while len(terms) > 1:
@@ -156,8 +162,7 @@
             ]
         )
     ]
-    for load in loads:
-        load.start()
+    loads[0].start()
 
     barrier = pltpu.get_barrier_semaphore()
     for off in range(1, n_ka):
@@ -168,6 +173,8 @@
         pl.semaphore_signal(
             barrier, inc=1, device_id=(ka, lax.rem(ta + off, n_ta)), device_id_type=MESH
         )
+    for load in loads[1:]:
+        load.start()
     loads[0].wait()
     for pair in range(ranks // 2):
         packed[pair // share, pair % share] = jnp.concatenate(
@@ -254,37 +261,34 @@
     loads[4].wait()
     mask(0)
 
-    groups = n_ka // GROUP
     second = []
-    home = lax.div(ka, GROUP)
-    for g in range(groups):
-        group = lax.rem(home + g, groups)
-        for i in range(GROUP):
-            source = group * GROUP + i
-
-            @pl.when(source != ka)
-            def _():
-                pltpu.make_async_remote_copy(
-                    src_ref=packed.at[ta],
-                    dst_ref=gathered.at[ta, source],
-                    send_sem=send1.at[0],
-                    recv_sem=recv1.at[source],
-                    device_id=(ka, lax.rem(ta + 1, n_ta)),
-                    device_id_type=MESH,
-                ).wait_recv()
-
+
+    def forward(source):
+        piece = gathered.at[ta, source]
         for off in range(1, n_ta):
-            piece = gathered.at[ta, pl.ds(group * GROUP, GROUP)]
             copy = pltpu.make_async_remote_copy(
                 src_ref=piece,
                 dst_ref=piece,
-                send_sem=send2.at[off, g],
-                recv_sem=recv2.at[ta, group],
+                send_sem=send2.at[off, source],
+                recv_sem=recv2.at[ta, source],
                 device_id=(ka, lax.rem(ta + off, n_ta)),
                 device_id_type=MESH,
             )
             copy.start()
             second.append(copy)
+
+    forward(ka)
+    for off in range(1, n_ka):
+        source = lax.rem(ka + off, n_ka)
+        pltpu.make_async_remote_copy(
+            src_ref=packed.at[ta],
+            dst_ref=gathered.at[ta, source],
+            send_sem=send1.at[off],
+            recv_sem=recv1.at[source],
+            device_id=(source, ta),
+            device_id_type=MESH,
+        ).wait_recv()
+        forward(source)
 
     for load in loads[5:]:
         load.wait()
@@ -325,8 +329,8 @@
 
     for off in range(1, n_ta):
         source = lax.rem(ta + off, n_ta)
-        for g in range(groups):
-            piece = gathered.at[source, pl.ds(g * GROUP, GROUP)]
+        for g in range(n_ka):
+            piece = gathered.at[source, g]
             pltpu.make_async_remote_copy(
                 src_ref=piece,
                 dst_ref=piece,
@@ -419,7 +423,6 @@
     oo = sigma_history.shape[2]
     no = math.isqrt(oo)
     share = ranks // 2 // n_ta
-    groups = n_ka // GROUP
     lengths = panel_lengths
     if n_ta > 2:
         lengths = lax.all_gather(panel_lengths, "ta", tiled=True)
@@ -455,8 +458,8 @@
             dma((2 * k_local + 1,)),
             dma((n_ka,)),
             dma((n_ka,)),
-            dma((n_ta, groups)),
-            dma((n_ta, groups)),
+            dma((n_ta, n_ka)),
+            dma((n_ta, n_ka)),
             dma((n_ta,)),
             dma((n_ta,)),
             dma((n_ta,)),
@@ -484,7 +487,7 @@
     green, ortho, coef = pl.pallas_call(
         finish,
         out_shape=outs,
-        in_specs=[hbm] * 3,
+        in_specs=[pl.BlockSpec(memory_space=pltpu.VMEM)] * 3,
         out_specs=(hbm, hbm, hbm),
         scratch_shapes=[dma((3,))],
         compiler_params=pltpu.CompilerParams(vmem_limit_bytes=8 * 1024 * 1024),

time: 28 us -> 21.1 us (0.75)
  Pallas kernels: 26.6 us -> 19.7 us
    pallas_call x1, Pallas kernels: 9.13 us -> 1.7 us  [body(): pl.pallas_call(finish, out_shape=outs, in_specs=[pl.BlockSpec(memory_spac...]
    pallas_call x1, Pallas kernels: 17.4 us -> 18 us  [body(): pl.pallas_call(functools.partial(kernel, n_ka, n_ta), out_shape=outs, in_...]
where the time goes in v4:
time: 21.1 us; the launch traced here: 21 us
  Pallas kernels  19.7 us (93%)
  between operations  1.29 us (6%)
    pallas_call x1, Pallas kernels, body(): pl.pallas_call(functools.partial(kernel, n_ka, n_ta), out_shape=outs, in_...  18 us
    pallas_call x1, Pallas kernels, body(): pl.pallas_call(finish, out_shape=outs, in_specs=[pl.BlockSpec(memory_spac...  1.7 us

profile of v4, /device:TPU:0, one launch (start us, length us, event | category | flops | bytes accessed | tf_op | source)
XLA Modules:
  0.0 21.0 jit_solution(3218408689533652792)
XLA Ops:
  1.3 18.0 %shard_map.112 = (f32[2,256]{1,0:T(2,128)}, f32[2,64,256]{2,1,0:T(8,128)}, f32[2,64,256]{2,1,0:T(8,128)}) custom-call(s32[1]{0:T(128)S(6)} %copy.12.length_ref, s32[2]{0:T(128)} %bitcast.4, f32[2,256]{1,0:T(2,128)} %green_hbm.1, f32[2,256]{1,0:T(2,128)} %ham_hbm.1, bf16[2,512,256]{2,1,0:T(8,128)(2,1)} %sigma_hbm.1, bf16[64,512]{1,0:T(8,128)(2,1)} %bitcast.3, ...), custom_call_target="tpu_custom_call" | custom-call | tf_op jit(solution)/shard_map/pallas_call | solution.py:437
  19.3 1.7 %shard_map.113 = (f32[2,256]{1,0:T(2,128)}, f32[2,64,256]{2,1,0:T(8,128)}, f32[2,64,256]{2,1,0:T(8,128)}) custom-call(f32[2,256]{1,0:T(2,128)} %get-tuple-element.9.green_ref, f32[2,64,256]{2,1,0:T(8,128)} %get-tuple-element.10.ortho_ref, f32[2,64,256]{2,1,0:T(8,128)} %get-tuple-element.11.coef_ref), custom_call_target="tpu_custom_call" | custom-call | tf_op jit(solution)/shard_map/pallas_call | solution.py:487

commit v5 on v3

--- a/solution.py
+++ b/solution.py
@@ -102,9 +102,6 @@
     hist_hbm,
     panel_hbm,
     sketch_hbm,
-    green_hbm_out,
-    ortho_hbm_out,
-    coef_hbm_out,
     green_out,
     ortho_out,
     coef_out,
@@ -122,7 +119,6 @@
     part,
     parts,
     local_sem,
-    out_sem,
     send1,
     recv1,
     send2,
@@ -156,8 +152,7 @@
             ]
         )
     ]
-    for load in loads:
-        load.start()
+    loads[0].start()
 
     barrier = pltpu.get_barrier_semaphore()
     for off in range(1, n_ka):
@@ -168,6 +163,8 @@
         pl.semaphore_signal(
             barrier, inc=1, device_id=(ka, lax.rem(ta + off, n_ta)), device_id_type=MESH
         )
+    for load in loads[1:]:
+        load.start()
     loads[0].wait()
     for pair in range(ranks // 2):
         packed[pair // share, pair % share] = jnp.concatenate(
@@ -190,7 +187,7 @@
         copy.start()
         first.append(copy)
 
-    panels, moves = [], []
+    panels = []
     for off in range(1, n_ta):
         copy = pltpu.make_async_remote_copy(
             src_ref=panel_hbm,
@@ -320,8 +317,6 @@
             green = green + STEP * (turn + integral)
         spread = jnp.where(own, jnp.concatenate([green] * (oo // 128), axis=1), 0.0)
         green_out[k : k + 1, :] = jnp.sum(spread, axis=0, keepdims=True)
-    moves.append(pltpu.make_async_copy(green_out, green_hbm_out, out_sem.at[2 * k_local]))
-    moves[-1].start()
 
     for off in range(1, n_ta):
         source = lax.rem(ta + off, n_ta)
@@ -372,33 +367,12 @@
             ortho = ortho[:rank] + ortho[rank:]
             if off == 0:
                 ortho_out[k] = ortho
-                move = pltpu.make_async_copy(ortho_out.at[k], ortho_hbm_out.at[k], out_sem.at[k])
-                move.start()
-                moves.append(move)
             piece = dot(ortho.astype(BF16), masked[off, k, :, mine])
             total = total + piece.astype(BF16).astype(F32)
         coef_out[k] = total
-        place = k_local + k
-        move = pltpu.make_async_copy(coef_out.at[k], coef_hbm_out.at[k], out_sem.at[place])
-        move.start()
-        moves.append(move)
 
     for copy in first + second + third + panels:
         copy.wait_send()
-    for move in moves:
-        move.wait()
-
-
-def finish(green_ref, ortho_ref, coef_ref, green_hbm, ortho_hbm, coef_hbm, sem):
-    moves = [
-        pltpu.make_async_copy(coef_ref, coef_hbm, sem.at[0]),
-        pltpu.make_async_copy(ortho_ref, ortho_hbm, sem.at[1]),
-        pltpu.make_async_copy(green_ref, green_hbm, sem.at[2]),
-    ]
-    for move in moves:
-        move.start()
-    for move in moves:
-        move.wait()
 
 
 def body(
@@ -424,6 +398,7 @@
     if n_ta > 2:
         lengths = lax.all_gather(panel_lengths, "ta", tiled=True)
     smem = pl.BlockSpec(memory_space=pltpu.SMEM)
+    vmem = pl.BlockSpec(memory_space=pltpu.VMEM)
     hbm = pl.BlockSpec(memory_space=pltpu.HBM)
     dma = pltpu.SemaphoreType.DMA
     outs = (
@@ -431,13 +406,12 @@
         jax.ShapeDtypeStruct((k_local, rank, rows), F32),
         jax.ShapeDtypeStruct((k_local, rank, cols // n_ta), F32),
     )
-    results = pl.pallas_call(
+    green, ortho, coef = pl.pallas_call(
         functools.partial(kernel, n_ka, n_ta),
         out_shape=outs,
         in_specs=[smem] + [hbm] * 8,
-        out_specs=(hbm, hbm, hbm),
+        out_specs=(vmem, vmem, vmem),
         scratch_shapes=[
-            *[pltpu.VMEM(x.shape, F32) for x in outs],
             pltpu.SMEM((k_local,), jnp.int32),
             pltpu.VMEM(green_now.shape, F32),
             pltpu.VMEM(green_now.shape, F32),
@@ -452,7 +426,6 @@
             pltpu.VMEM((k_local, no, 128), F32),
             pltpu.VMEM((n_ta, k_local, no, 128), F32),
             dma((8,)),
-            dma((2 * k_local + 1,)),
             dma((n_ka,)),
             dma((n_ka,)),
             dma((n_ta, groups)),
@@ -481,14 +454,6 @@
             )
         ],
     )
-    green, ortho, coef = pl.pallas_call(
-        finish,
-        out_shape=outs,
-        in_specs=[hbm] * 3,
-        out_specs=(hbm, hbm, hbm),
-        scratch_shapes=[dma((3,))],
-        compiler_params=pltpu.CompilerParams(vmem_limit_bytes=8 * 1024 * 1024),
-    )(*[pltpu.with_memory_space_constraint(x, pltpu.HBM) for x in results])
     return green, ortho.transpose(0, 2, 1), coef
 
 

time: 28 us -> 22.5 us (0.80)
  Pallas kernels: 26.6 us -> 17.5 us
  local copies, waits for them, and re-layouts: 0 us -> 3.51 us
    pallas_call x1 -> x0, Pallas kernels: 9.13 us -> none  [body(): pl.pallas_call(finish, out_shape=outs, in_specs=[hbm] * 3, out_specs=(hbm...]
    unnamed x0 -> x7, local copies, waits for them, and re-layouts: none -> 3.51 us
where the time goes in v5:
time: 22.5 us; the launch traced here: 22.3 us
  Pallas kernels  17.5 us (78%)
  local copies, waits for them, and re-layouts  3.51 us (16%)
  between operations  1.3 us (6%)
    pallas_call x1, Pallas kernels, body(): pl.pallas_call(functools.partial(kernel, n_ka, n_ta), out_shape=outs, in_...  17.5 us
    unnamed x7, local copies, waits for them, and re-layouts  3.51 us

profile of v5, /device:TPU:0, one launch (start us, length us, event | category | flops | bytes accessed | tf_op | source)
XLA Modules:
  0.0 22.3 jit_solution(10629174080858404040)
XLA Ops:
  1.3 17.5 %shard_map.112 = (f32[2,256]{1,0:T(2,128)}, f32[2,64,256]{2,1,0:T(8,128)}, f32[2,64,256]{2,1,0:T(8,128)}) custom-call(s32[1]{0:T(128)S(6)} %copy.15.length_ref, s32[2]{0:T(128)} %bitcast.5, f32[2,256]{1,0:T(2,128)} %green_hbm.1, f32[2,256]{1,0:T(2,128)} %ham_hbm.1, bf16[2,512,256]{2,1,0:T(8,128)(2,1)} %sigma_hbm.1, bf16[64,512]{1,0:T(8,128)(2,1)} %bitcast.4, ...), custom_call_target="tpu_custom_call" | custom-call | tf_op jit(solution)/shard_map/pallas_call | solution.py:409
  18.8 0.0 copy-start.1
  18.8 0.7 %copy-done.1 = f32[2,256]{1,0:T(2,128)S(1)} copy-done((f32[2,256]{1,0:T(2,128)S(1)}, f32[2,256]{1,0:T(2,128)}, u32[]{:S(2)}) %copy-start.1) | copy-done | bytes 2072
  19.4 0.6 %copy.16 = f32[2,256]{1,0:T(2,128)} copy(f32[2,256]{1,0:T(2,128)S(1)} %copy-done.1) | data formatting | bytes 4096
  20.0 0.0 copy-start
  20.0 1.6 %copy.17 = f32[2,256,64]{1,2,0:T(8,128)} copy(f32[2,256,64]{1,2,0:T(8,128)} %bitcast.3) | data formatting | bytes 262144
  21.6 0.0 copy-done
  21.6 0.7 %copy.18 = f32[2,64,256]{2,1,0:T(8,128)} copy(f32[2,64,256]{2,1,0:T(8,128)S(1)} %copy-done) | data formatting | bytes 262144
Async XLA Ops:
  18.8 0.7 %copy-start.1 = (f32[2,256]{1,0:T(2,128)S(1)}, f32[2,256]{1,0:T(2,128)}, u32[]{:S(2)}) copy-start(f32[2,256]{1,0:T(2,128)} %get-tuple-element.12) | copy-start | bytes 6148
  20.0 1.6 %copy-start = (f32[2,64,256]{2,1,0:T(8,128)S(1)}, f32[2,64,256]{2,1,0:T(8,128)}, u32[]{:S(2)}) copy-start(f32[2,64,256]{2,1,0:T(8,128)} %get-tuple-element.14) | copy-start | bytes 393220

commit v6 on v5

--- a/solution.py
+++ b/solution.py
@@ -436,7 +436,7 @@
             dma((n_ta,)),
         ],
         compiler_params=pltpu.CompilerParams(
-            collective_id=0, has_side_effects=True, vmem_limit_bytes=56 * 1024 * 1024
+            collective_id=0, has_side_effects=True, vmem_limit_bytes=48 * 1024 * 1024
         ),
     )(
         lengths,

time: 22.5 us -> 20.1 us (0.89)
  local copies, waits for them, and re-layouts: 3.51 us -> 1.89 us
  Pallas kernels: 17.5 us -> 16.8 us
    unnamed x7 -> x3, local copies, waits for them, and re-layouts: 3.51 us -> 1.89 us
    pallas_call x1, Pallas kernels: 17.5 us -> 16.8 us  [body(): pl.pallas_call(functools.partial(kernel, n_ka, n_ta), out_shape=outs, in_...]
where the time goes in v6:
time: 20.1 us; the launch traced here: 20 us
  Pallas kernels  16.8 us (84%)
  local copies, waits for them, and re-layouts  1.89 us (9%)
  between operations  1.29 us (6%)
    pallas_call x1, Pallas kernels, body(): pl.pallas_call(functools.partial(kernel, n_ka, n_ta), out_shape=outs, in_...  16.8 us
    unnamed x3, local copies, waits for them, and re-layouts  1.89 us

profile of v6, /device:TPU:0, one launch (start us, length us, event | category | flops | bytes accessed | tf_op | source)
XLA Modules:
  0.0 20.0 jit_solution(1210173606777553235)
XLA Ops:
  1.3 16.8 %shard_map.112 = (f32[2,256]{1,0:T(2,128)S(1)}, f32[2,64,256]{2,1,0:T(8,128)S(1)}, f32[2,64,256]{2,1,0:T(8,128)S(1)}) custom-call(s32[1]{0:T(128)S(6)} %copy.15.length_ref, s32[2]{0:T(128)} %bitcast.5, f32[2,256]{1,0:T(2,128)} %green_hbm.1, f32[2,256]{1,0:T(2,128)} %ham_hbm.1, bf16[2,512,256]{2,1,0:T(8,128)(2,1)} %sigma_hbm.1, bf16[64,512]{1,0:T(8,128)(2,1)} %bitcast.4, ...), custom_call_target="tpu_custom_call" | custom-call | tf_op jit(solution)/shard_map/pallas_call | solution.py:409
  18.1 0.6 %copy.16 = f32[2,256]{1,0:T(2,128)} copy(f32[2,256]{1,0:T(2,128)S(1)} %get-tuple-element.12) | data formatting | bytes 4096
  18.7 0.7 %copy.17 = f32[2,256,64]{1,2,0:T(8,128)} copy(f32[2,256,64]{1,2,0:T(8,128)S(1)} %bitcast.3) | data formatting | bytes 262144
  19.3 0.7 %copy.18 = f32[2,64,256]{2,1,0:T(8,128)} copy(f32[2,64,256]{2,1,0:T(8,128)S(1)} %get-tuple-element.14) | data formatting | bytes 262144
